TPU v7x, 32 devices: a whole 2x2x4 slice. The times are simulated.
32 devices in a mesh: seq: 8 (over z, x), ch: 4 (over y, core).
Axes of the slice: x: 2, y: 2, z: 4, core: 2. Of those that a mesh axis runs over, the one named last changes fastest.
Arguments:
- block_input: bfloat16 [8192, 2048], P('ch', 'seq'), may hold values from -110 to 110
- norm_gain: float32 [8192], P('ch'), may hold values from 0.1 to 1.9
- short_taps: bfloat16 [8192, 7], P('ch'), may hold values from -2 to 2
- medium_taps: bfloat16 [8192, 128], P('ch'), may hold values from -0.5 to 0.5
- long_filter: float32 [8192, 2048], P(('ch', 'seq')), may hold values from -2 to 2
- grad_out: bfloat16 [8192, 2048], P('ch', 'seq'), may hold values from -2.390625 to 2.390625
Outputs:
- grad_normed: bfloat16 [8192, 2048], P('ch', 'seq')
- grad_long: float32 [8192, 2048], P(('ch', 'seq'))
- grad_medium: float32 [8192, 128], P(('ch', 'seq'))
- grad_short: float32 [8192, 7], P(('ch', 'seq'))
All inputs are finite; a program needn't handle non-finite values.
Results may differ from a plain program's by a relative error of at most 0.0058.
Values may be sent and summed in bfloat16 or wider, within the bound.
A program may use at most 128 MiB of HBM per device.

v0:
```python
import math
import jax
import jax.numpy as jnp
from jax import lax
from jax.sharding import PartitionSpec as P

highest = lax.Precision.HIGHEST


def depthwise(signal, taps):
    result = lax.conv_general_dilated(
        signal[None],
        taps[:, None, :],
        (1,),
        "VALID",
        dimension_numbers=("NCH", "OIH", "NCH"),
        feature_group_count=signal.shape[0],
        preferred_element_type=jnp.float32,
    )
    return result[0]


def fourier_tables(length):
    total = 2 * length
    inner = 128
    outer = total // inner
    half = outer // 2
    two_pi = 2.0 * math.pi
    freq_outer = jnp.arange(outer, dtype=jnp.int32)
    pos_half = jnp.arange(half, dtype=jnp.int32)
    pos_inner = jnp.arange(inner, dtype=jnp.int32)
    outer_angle = (
        two_pi * (freq_outer[:, None] * pos_half[None, :] % outer).astype(jnp.float32) / outer
    )
    inner_angle = (
        two_pi * (pos_inner[:, None] * pos_inner[None, :] % inner).astype(jnp.float32) / inner
    )
    twist_angle = (
        two_pi * (freq_outer[:, None] * pos_inner[None, :] % total).astype(jnp.float32) / total
    )
    return (
        jnp.cos(outer_angle),
        jnp.sin(outer_angle),
        jnp.cos(inner_angle),
        jnp.sin(inner_angle),
        jnp.cos(twist_angle),
        jnp.sin(twist_angle),
    )


def forward_dft(signal, tables):
    cos_outer, sin_outer, cos_inner, sin_inner, cos_twist, sin_twist = tables
    blocks = signal.reshape(signal.shape[0], cos_outer.shape[1], cos_inner.shape[0])
    real = jnp.einsum("kn,cnq->ckq", cos_outer, blocks, precision=highest)
    imag = -jnp.einsum("kn,cnq->ckq", sin_outer, blocks, precision=highest)
    turned_re = real * cos_twist + imag * sin_twist
    turned_im = imag * cos_twist - real * sin_twist
    out_re = jnp.einsum("ckq,qr->ckr", turned_re, cos_inner, precision=highest) + jnp.einsum(
        "ckq,qr->ckr", turned_im, sin_inner, precision=highest
    )
    out_im = jnp.einsum("ckq,qr->ckr", turned_im, cos_inner, precision=highest) - jnp.einsum(
        "ckq,qr->ckr", turned_re, sin_inner, precision=highest
    )
    return (out_re, out_im)


def inverse_dft(spec_re, spec_im, tables):
    cos_outer, sin_outer, cos_inner, sin_inner, cos_twist, sin_twist = tables
    total = cos_outer.shape[0] * cos_inner.shape[0]
    step_re = jnp.einsum("ckq,qr->ckr", spec_re, cos_inner, precision=highest) - jnp.einsum(
        "ckq,qr->ckr", spec_im, sin_inner, precision=highest
    )
    step_im = jnp.einsum("ckq,qr->ckr", spec_im, cos_inner, precision=highest) + jnp.einsum(
        "ckq,qr->ckr", spec_re, sin_inner, precision=highest
    )
    turned_re = step_re * cos_twist - step_im * sin_twist
    turned_im = step_im * cos_twist + step_re * sin_twist
    blocks = jnp.einsum("kn,ckq->cnq", cos_outer, turned_re, precision=highest) - jnp.einsum(
        "kn,ckq->cnq", sin_outer, turned_im, precision=highest
    )
    return (blocks / total).reshape(spec_re.shape[0], -1)


def on_device(block_input, norm_gain, short_taps, medium_taps, long_filter, grad_out):
    chans, tokens = block_input.shape
    seq_count = lax.axis_size("seq")
    med_count = medium_taps.shape[1]
    reach = med_count + short_taps.shape[1] - 2
    inputs32 = block_input.astype(jnp.float32)
    squares = lax.psum(jnp.sum(inputs32 * inputs32, axis=0), "ch")
    inv_rms = lax.rsqrt(squares / (chans * lax.axis_size("ch")) + 1e-05)
    normed = (inputs32 * inv_rms[None, :] * norm_gain[:, None]).astype(jnp.bfloat16)
    arrived, grad_chan = (
        lax.all_to_all(normed, "seq", split_axis=0, concat_axis=1, tiled=True),
        lax.all_to_all(grad_out, "seq", split_axis=0, concat_axis=1, tiled=True),
    )
    group, length = arrived.shape
    scale = length ** (-0.5)
    offset = lax.axis_index("seq") * group
    short_local = lax.dynamic_slice_in_dim(short_taps, offset, group, 0)
    medium_local = lax.dynamic_slice_in_dim(medium_taps, offset, group, 0)
    normed_pad = jnp.pad(arrived, ((0, 0), (reach, 0)))
    shorted_pad = depthwise(normed_pad, short_local[:, ::-1]).astype(jnp.bfloat16)
    filtered_chan = depthwise(shorted_pad, medium_local[:, ::-1]).astype(jnp.bfloat16)
    tables = fourier_tables(length)
    grad_re, grad_im = forward_dft(grad_chan.astype(jnp.float32), tables)
    filt_re, filt_im = forward_dft(long_filter, tables)
    sig_re, sig_im = forward_dft(filtered_chan.astype(jnp.float32), tables)
    grad_filtered = inverse_dft(
        filt_re * grad_re + filt_im * grad_im, filt_re * grad_im - filt_im * grad_re, tables
    ).astype(jnp.bfloat16)
    grad_long = (
        inverse_dft(
            sig_re * grad_re + sig_im * grad_im, sig_re * grad_im - sig_im * grad_re, tables
        )
        * scale
    )
    back_pad = jnp.pad(grad_filtered, ((0, 0), (0, reach)))
    shorted_grad = depthwise(back_pad, medium_local).astype(jnp.bfloat16)
    normed_grad = depthwise(shorted_grad, short_local).astype(jnp.bfloat16)
    medium_local_grad = depthwise(shorted_pad, grad_filtered)[:, ::-1] * scale
    short_local_grad = (
        depthwise(normed_pad[:, med_count - 1 :], shorted_grad[:, :length])[:, ::-1] * scale
    )
    leaving = normed_grad.reshape(group, seq_count, tokens)
    returned = lax.all_to_all(leaving, "seq", split_axis=1, concat_axis=0, tiled=True).reshape(
        chans, -1
    )
    return (returned, grad_long, medium_local_grad, short_local_grad)


def solution(mesh):
    placed = (
        P("ch", "seq"),
        P("ch"),
        P("ch", None),
        P("ch", None),
        P(("ch", "seq"), None),
        P("ch", "seq"),
    )
    return jax.shard_map(
        on_device,
        mesh=mesh,
        in_specs=placed,
        out_specs=(
            P("ch", "seq"),
            P(("ch", "seq"), None),
            P(("ch", "seq"), None),
            P(("ch", "seq"), None),
        ),
        check_vma=False,
    )
```

profile of v0, /device:TPU:0, one launch (start us, length us, event | category | flops | bytes accessed | tf_op | source)
XLA Modules:
  0.0 433.6 jit_solution(14907793232586408200)
XLA Ops:
  0.6 1.6 fusion.44
  2.2 8.4 %psum.7 = f32[256]{0:T(256)S(1)} all-reduce(f32[256]{0:T(256)S(1)} %fusion.44), channel_id=1, replica_groups=mesh['seq'=8,'ch'=4] {'ch'}, use_global_device_ids=true, to_apply=%region_1.0 | all-reduce | flops 256 | bytes 2048 | tf_op jit(solution)/shard_map/psum | solution.py:90
  10.6 1.6 fusion.46
  12.2 1.3 copy.122
  13.5 5.8 %all-to-all-start.2 = ((bf16[8,256,256]{1,2,0:T(8,128)(2,1)}), bf16[8,256,256]{1,2,0:T(8,128)(2,1)}, u32[]{:S(2)}, u32[]{:S(2)}) async-start(bf16[8,256,256]{1,2,0:T(8,128)(2,1)} %copy.122), calls=%async_computation.2 | async-start | bytes 2097152 | tf_op jit(solution)/shard_map/all_to_all | solution.py:94
  20.1 2.0 copy.147
  23.2 1.3 fusion.345
  24.6 5.1 %fusion.171 = f32[32,256,128]{2,0,1:T(8,128)} fusion(f32[256,16,128]{2,1,0:T(8,128)S(1)} %bitcast.202), kind=kOutput, calls=%fused_computation.179 | convolution fusion | flops 201333760 | bytes 6291456 | tf_op jit(solution)/shard_map/kn,cnq->ckq/dot_general | solution.py:54
  29.7 5.1 %fusion.163 = f32[32,256,128]{2,0,1:T(8,128)} fusion(f32[256,16,128]{2,1,0:T(8,128)S(1)} %bitcast.203), kind=kOutput, calls=%fused_computation.171 | convolution fusion | flops 201333760 | bytes 6291456 | tf_op jit(solution)/shard_map/kn,cnq->ckq/dot_general | solution.py:55
  34.9 9.3 %all-to-all-done.2 = bf16[8,256,256]{1,2,0:T(8,128)(2,1)} async-done(((bf16[8,256,256]{1,2,0:T(8,128)(2,1)}), bf16[8,256,256]{1,2,0:T(8,128)(2,1)}, u32[]{:S(2)}, u32[]{:S(2)}) %all-to-all-start.2) | async-done | bytes 1048608 | tf_op jit(solution)/shard_map/all_to_all | solution.py:94
  44.2 4.2 all-to-all-start
  48.4 1.5 pad_bitcast_fusion.1
  50.6 2.8 select_convert_fusion
  53.4 0.9 select_bitcast_fusion
  54.4 24.1 %fusion.66 = bf16[8,273,256]{2,0,1:T(8,128)(2,1)S(1)} fusion(bf16[256,1,128]{0,1,2:T(2,128)(2,1)S(1)} %copy.126, bf16[1,7,127,256]{3,1,2,0:T(8,128)(2,1)S(1)} %slice.20, bf16[1,8,273,256]{3,1,2,0:T(8,128)(2,1)S(1)} %select_bitcast_fusion), kind=kOutput, calls=%fused_computation.86 | convolution fusion | flops 148604928 | bytes 2757120 | tf_op jit(solution)/shard_map/conv_general_dilated | solution.py:11
  79.1 1.0 slice.21
  80.2 1.9 copy.142
  82.1 3.8 fusion.166
  85.9 3.9 fusion.158
  89.8 1.8 copy.106
  91.6 1.2 reshape.87
  92.8 3.2 fusion.161
  96.1 6.0 %add_bitcast_fusion = (f32[256,32,128]{2,1,0:T(8,128)S(1)}, f32[256,32,128]{2,1,0:T(8,128)S(1)}, f32[256,32,128]{2,1,0:T(8,128)S(1)}, f32[256,32,128]{2,1,0:T(8,128)S(1)}) fusion(f32[32,256,128]{2,0,1:T(8,128)S(1)} %fusion.161, f32[32,128]{1,0:T(8,128)S(1)} %get-tuple-element.38, f32[32,128]{1,0:T(8,128)S(1)} %get-tuple-element.39, ...), kind=kOutput, calls=%fused_computation.24 | convolution fusion | flops 216013824 | bytes 30441472 | tf_op jit(solution)/shard_map/kn,cnq->ckq/dot_general | solution.py:54
  102.1 8.6 %fusion.12 = f32[256,32,128]{2,0,1:T(8,128)} fusion(f32[256,32,128]{2,1,0:T(8,128)S(1)} %get-tuple-element.29), kind=kOutput, calls=%fused_computation.29 | convolution fusion | flops 1610842112 | bytes 8388608 | tf_op jit(solution)/shard_map/ckq,qr->ckr/dot_general | solution.py:58
  110.7 6.8 %fusion.10 = f32[256,32,128]{2,0,1:T(8,128)S(1)} fusion(f32[256,32,128]{2,1,0:T(8,128)S(1)} %get-tuple-element.29), kind=kOutput, calls=%fused_computation.27 | convolution fusion | flops 1610842112 | bytes 8388608 | tf_op jit(solution)/shard_map/ckq,qr->ckr/dot_general | solution.py:61
  117.5 7.2 %fusion.18 = f32[256,32,128]{2,0,1:T(8,128)S(1)} fusion(f32[256,32,128]{2,1,0:T(8,128)S(1)} %get-tuple-element.36), kind=kOutput, calls=%fused_computation.35 | convolution fusion | flops 1610842112 | bytes 8388608 | tf_op jit(solution)/shard_map/ckq,qr->ckr/dot_general | solution.py:61
  124.7 7.1 %fusion.20 = f32[256,32,128]{2,0,1:T(8,128)S(1)} fusion(f32[256,32,128]{2,1,0:T(8,128)S(1)} %get-tuple-element.36), kind=kOutput, calls=%fused_computation.37 | convolution fusion | flops 1610842112 | bytes 8388608 | tf_op jit(solution)/shard_map/ckq,qr->ckr/dot_general | solution.py:58
  131.8 13.2 %fusion.92 = f32[256,32,128]{2,0,1:T(8,128)} fusion(f32[256,128,32]{1,2,0:T(8,128)S(1)} %copy-done.2, f32[256,128,32]{1,2,0:T(8,128)S(1)} %copy-done.3, f32[32,128]{1,0:T(8,128)S(1)} %get-tuple-element.38, f32[32,128]{1,0:T(8,128)S(1)} %get-tuple-element.39), kind=kOutput, calls=%fused_computation.109 | convolution fusion | flops 1615036416 | bytes 12615680 | tf_op jit(solution)/shard_map/ckq,qr->ckr/dot_general | solution.py:58
  145.0 12.9 %fusion.88 = f32[256,32,128]{2,0,1:T(8,128)} fusion(f32[256,128,32]{1,2,0:T(8,128)S(1)} %copy-done.2, f32[256,128,32]{1,2,0:T(8,128)S(1)} %copy-done.3, f32[32,128]{1,0:T(8,128)S(1)} %get-tuple-element.38, f32[32,128]{1,0:T(8,128)S(1)} %get-tuple-element.39), kind=kOutput, calls=%fused_computation.108 | convolution fusion | flops 1615036416 | bytes 12615680 | tf_op jit(solution)/shard_map/ckq,qr->ckr/dot_general | solution.py:61
  158.0 1.2 copy.133
  159.2 14.5 %convolution_add_fusion.1 = f32[256,32,128]{2,0,1:T(8,128)} fusion(f32[256,32,128]{2,0,1:T(8,128)} %fusion.92, f32[256,128,32]{1,2,0:T(8,128)S(1)} %copy-done.2, f32[256,128,32]{1,2,0:T(8,128)S(1)} %copy-done.3, f32[32,128]{1,0:T(8,128)S(1)} %get-tuple-element.38, f32[32,128]{1,0:T(8,128)S(1)} %get-tuple-element.39), kind=kOutput, calls=%fused_computation.62 | convolution fusion | flops 1616084992 | bytes 16809984 | tf_op jit(solution)/shard_map/ckq,qr->ckr/dot_general | solution.py:58
  173.7 8.4 %fusion.36 = f32[256,32,128]{2,0,1:T(8,128)} fusion(f32[256,32,128]{2,0,1:T(8,128)S(1)} %copy-done.8, f32[256,32,128]{2,1,0:T(8,128)S(1)} %get-tuple-element.28), kind=kOutput, calls=%fused_computation.57 | convolution fusion | flops 1611890688 | bytes 12582912 | tf_op jit(solution)/shard_map/ckq,qr->ckr/dot_general | solution.py:58
  182.1 8.6 %fusion.39 = f32[256,32,128]{2,0,1:T(8,128)} fusion(f32[256,32,128]{2,0,1:T(8,128)S(1)} %fusion.10, f32[256,32,128]{2,1,0:T(8,128)S(1)} %get-tuple-element.28), kind=kOutput, calls=%fused_computation.58 | convolution fusion | flops 1611890688 | bytes 12582912 | tf_op jit(solution)/shard_map/ckq,qr->ckr/dot_general | solution.py:61
  190.7 8.6 %fusion.33 = f32[256,32,128]{2,0,1:T(8,128)} fusion(f32[256,32,128]{2,0,1:T(8,128)S(1)} %fusion.18, f32[256,32,128]{2,1,0:T(8,128)S(1)} %get-tuple-element.37), kind=kOutput, calls=%fused_computation.56 | convolution fusion | flops 1611890688 | bytes 12582912 | tf_op jit(solution)/shard_map/ckq,qr->ckr/dot_general | solution.py:61
  199.3 8.4 %fusion.30 = f32[256,32,128]{2,0,1:T(8,128)} fusion(f32[256,32,128]{2,0,1:T(8,128)S(1)} %fusion.20, f32[256,32,128]{2,1,0:T(8,128)S(1)} %get-tuple-element.37), kind=kOutput, calls=%fused_computation.55 | convolution fusion | flops 1611890688 | bytes 12582912 | tf_op jit(solution)/shard_map/ckq,qr->ckr/dot_general | solution.py:58
  207.7 22.7 %multiply_subtract_fusion.1 = (f32[256,32,128]{2,0,1:T(8,128)}, f32[256,32,128]{2,0,1:T(8,128)}, f32[256,32,128]{2,0,1:T(8,128)}, f32[256,32,128]{2,0,1:T(8,128)}) fusion(f32[256,32,128]{2,0,1:T(8,128)} %fusion.36, f32[256,32,128]{2,0,1:T(8,128)} %convolution_add_fusion.1, f32[256,32,128]{2,0,1:T(8,128)} %fusion.39, f32[256,32,128]{2,0,1:T(8,128)} %fusion.33, ...), kind=kOutput, calls=%fused_computation.17 | convolution fusion | flops 1628667904 | bytes 50364416 | tf_op jit(solution)/shard_map/ckq,qr->ckr/dot_general | solution.py:61
  230.4 6.0 %fusion.111 = f32[256,32,128]{2,0,1:T(8,128)S(1)} fusion(f32[256,32,128]{2,0,1:T(8,128)} %get-tuple-element.21), kind=kOutput, calls=%fused_computation.131 | convolution fusion | flops 1610842112 | bytes 8388608 | tf_op jit(solution)/shard_map/ckq,qr->ckr/dot_general | solution.py:70
  236.5 5.6 %fusion.109 = f32[256,32,128]{2,0,1:T(8,128)} fusion(f32[256,32,128]{2,0,1:T(8,128)S(1)} %copy-done.6), kind=kOutput, calls=%fused_computation.129 | convolution fusion | flops 1610842112 | bytes 8388608 | tf_op jit(solution)/shard_map/ckq,qr->ckr/dot_general | solution.py:73
  242.1 3.8 convolution_subtract_fusion
  245.9 3.8 fusion.117
  249.7 3.8 fusion.115
  253.5 4.2 convolution_subtract_fusion.2
  257.7 5.5 %convolution_add_fusion.2 = f32[256,32,128]{2,0,1:T(8,128)} fusion(f32[256,32,128]{2,0,1:T(8,128)S(1)} %fusion.115, f32[256,32,128]{2,0,1:T(8,128)S(1)} %copy-done.4), kind=kOutput, calls=%fused_computation.63 | convolution fusion | flops 1611890688 | bytes 12582912 | tf_op jit(solution)/shard_map/ckq,qr->ckr/dot_general | solution.py:73
  263.3 11.6 %multiply_subtract_fusion = (f32[256,32,128]{2,0,1:T(8,128)}, f32[256,32,128]{2,0,1:T(8,128)}, f32[256,32,128]{2,0,1:T(8,128)}, f32[256,32,128]{2,0,1:T(8,128)}) fusion(f32[256,32,128]{2,0,1:T(8,128)S(1)} %convolution_subtract_fusion, f32[32,128]{1,0:T(8,128)S(1)} %get-tuple-element.38, f32[32,128]{1,0:T(8,128)S(1)} %get-tuple-element.39, ...), kind=kOutput, calls=%fused_computation.16 | convolution fusion | flops 1624473600 | bytes 37781504 | tf_op jit(solution)/shard_map/ckq,qr->ckr/dot_general | solution.py:73
  274.9 7.0 %fusion.6 = f32[256,128,16]{1,2,0:T(8,128)S(1)} fusion(f32[256,32,128]{2,0,1:T(8,128)} %get-tuple-element.34), kind=kOutput, calls=%fused_computation.11 | convolution fusion | flops 201333760 | bytes 6291456 | tf_op jit(solution)/shard_map/kn,ckq->cnq/dot_general | solution.py:78
  281.9 4.9 %fusion.69 = bf16[256,16,128]{2,1,0:T(8,128)(2,1)S(1)} fusion(f32[256,128,16]{1,2,0:T(8,128)S(1)} %fusion.6, f32[256,32,128]{2,0,1:T(8,128)S(1)} %copy-done.10), kind=kOutput, calls=%fused_computation.88 | convolution fusion | flops 202906624 | bytes 7340032 | tf_op jit(solution)/shard_map/kn,ckq->cnq/dot_general | solution.py:78
  287.6 1.3 convert_element_type.181
  289.9 28.6 %select_convert_fusion.1 = bf16[8,273,256]{2,0,1:T(8,128)(2,1)S(1)} fusion(bf16[256,1,128]{0,1,2:T(2,128)(2,1)S(1)} %copy-done.14, bf16[256,1,7,127]{0,2,3,1:T(8,128)(2,1)S(1)} %slice.16, bf16[256,1,8,273]{0,2,3,1:T(8,128)(2,1)S(1)} %copy.117, pred[8,273]{0,1:T(8,128)(4,1)S(1)} %copy-done.15), kind=kOutput, calls=%fused_computation.54 | convolution fusion | flops 149164032 | bytes 2759304 | tf_op jit(solution)/shard_map/conv_general_dilated | solution.py:11
  318.5 0.9 select_bitcast_fusion.1
  319.4 1.2 copy.136
  320.7 2.4 convolution_convert_fusion
  323.7 1.0 slice.18
  324.7 5.9 %all-to-all-start.1 = ((bf16[256,8,256]{0,2,1:T(8,128)(2,1)}), bf16[256,8,256]{0,2,1:T(8,128)(2,1)}, u32[]{:S(2)}, u32[]{:S(2)}) async-start(bf16[256,8,256]{0,2,1:T(8,128)(2,1)} %bitcast.19), calls=%async_computation.1 | async-start | bytes 2097152 | tf_op jit(solution)/shard_map/all_to_all | solution.py:126
  330.6 6.8 %fusion.2 = f32[256,128,16]{1,2,0:T(8,128)S(1)} fusion(f32[256,32,128]{2,0,1:T(8,128)} %get-tuple-element.25), kind=kOutput, calls=%fused_computation.6 | convolution fusion | flops 201333760 | bytes 6291456 | tf_op jit(solution)/shard_map/kn,ckq->cnq/dot_general | solution.py:78
  337.5 6.5 %reshape.129 = bf16[1,2184,256]{2,0,1:T(2,128)(2,1)} reshape(bf16[8,273,256]{2,1,0:T(8,128)(2,1)} %copy.133) | data formatting | bytes 2236416 | tf_op jit(solution)/shard_map/convert_element_type | solution.py:103
  343.9 5.9 %copy.135 = bf16[256,1,2048]{0,1,2:T(2,128)(2,1)} copy(bf16[256,1,2048]{2,0,1:T(8,128)(2,1)} %convert_element_type.181) | data formatting | bytes 2097152 | tf_op jit(solution)/shard_map/convert_element_type | solution.py:111
  349.9 25.4 %fusion.326 = f32[1,256,128]{1,0,2:T(1,128)S(1)} fusion(bf16[1,2184,256]{2,0,1:T(2,128)(2,1)} %reshape.129, bf16[256,1,2048]{0,1,2:T(2,128)(2,1)} %copy.135), kind=kOutput, calls=%fused_computation.326 | convolution fusion | flops 134217728 | bytes 2297856 | tf_op jit(solution)/shard_map/conv_general_dilated | solution.py:11
  375.4 2.6 reshape.95
  378.0 2.3 slice_bitcast_fusion
  380.3 6.9 %subtract_multiply_fusion = f32[256,128,16]{1,2,0:T(8,128)S(1)} fusion(f32[256,128,16]{1,2,0:T(8,128)S(1)} %fusion.2, f32[256,32,128]{2,0,1:T(8,128)} %get-tuple-element.24), kind=kOutput, calls=%fused_computation.72 | convolution fusion | flops 202382336 | bytes 8388608 | tf_op jit(solution)/shard_map/kn,ckq->cnq/dot_general | solution.py:78
  387.2 2.2 copy.217
  390.2 1.5 slice_bitcast_fusion.1
  391.8 38.4 %fusion.42 = f32[1,256,7]{1,0,2:T(1,128)S(1)} fusion(bf16[1,256,2054]{1,2,0:T(8,128)(2,1)S(1)} %slice_bitcast_fusion.1, bf16[256,1,2048]{0,2,1:T(8,128)(2,1)S(1)} %slice_bitcast_fusion.2), kind=kOutput, calls=%fused_computation.65 | convolution fusion | flops 7340032 | bytes 2107392 | tf_op jit(solution)/shard_map/conv_general_dilated | solution.py:11
  430.9 2.3 copy.121
  (71 shorter events, 7.3 us)
Async XLA Ops:
  0.6 18.7 %copy-start = (bf16[2048,128]{1,0:T(8,128)(2,1)S(1)}, bf16[2048,128]{1,0:T(8,128)(2,1)}, u32[]{:S(2)}) copy-start(bf16[2048,128]{1,0:T(8,128)(2,1)} %param.9) | copy-start | bytes 1572868
  13.5 30.7 %all-to-all-start.2 = ((bf16[8,256,256]{1,2,0:T(8,128)(2,1)}), bf16[8,256,256]{1,2,0:T(8,128)(2,1)}, u32[]{:S(2)}, u32[]{:S(2)}) async-start(bf16[8,256,256]{1,2,0:T(8,128)(2,1)} %copy.122), calls=%async_computation.2 | async-start | bytes 2097152 | tf_op jit(solution)/shard_map/all_to_all | solution.py:94
  44.2 45.7 %all-to-all-start = ((bf16[8,256,256]{2,1,0:T(8,128)(2,1)}), bf16[8,256,256]{2,1,0:T(8,128)(2,1)}, u32[]{:S(2)}, u32[]{:S(2)}) async-start(bf16[8,256,256]{2,1,0:T(8,128)(2,1)} %bitcast.210), calls=%async_computation | async-start | bytes 2097152 | tf_op jit(solution)/shard_map/all_to_all | solution.py:95
  48.4 2.2 copy-start.16
  53.4 25.2 %copy-start.11 = (bf16[8,273,256]{2,0,1:T(8,128)(2,1)}, bf16[8,273,256]{2,0,1:T(8,128)(2,1)S(1)}, u32[]{:S(2)}) copy-start(bf16[8,273,256]{2,0,1:T(8,128)(2,1)S(1)} %select_convert_fusion) | copy-start | bytes 3354628
  92.8 3.3 copy-start.9
  124.7 7.1 %copy-start.2 = (f32[256,128,32]{1,2,0:T(8,128)S(1)}, f32[256,128,32]{1,2,0:T(8,128)}, u32[]{:S(2)}) copy-start(f32[256,128,32]{1,2,0:T(8,128)} %fusion.166) | copy-start | bytes 12582916
  124.7 7.1 %copy-start.3 = (f32[256,128,32]{1,2,0:T(8,128)S(1)}, f32[256,128,32]{1,2,0:T(8,128)}, u32[]{:S(2)}) copy-start(f32[256,128,32]{1,2,0:T(8,128)} %fusion.158) | copy-start | bytes 12582916
  145.0 12.9 %copy-start.12 = (bf16[8,273,256]{2,0,1:T(8,128)(2,1)S(1)}, bf16[8,273,256]{2,0,1:T(8,128)(2,1)}, u32[]{:S(2)}) copy-start(bf16[8,273,256]{2,0,1:T(8,128)(2,1)} %copy-done.11) | copy-start | bytes 3354628
  159.2 14.5 %copy-start.8 = (f32[256,32,128]{2,0,1:T(8,128)S(1)}, f32[256,32,128]{2,0,1:T(8,128)}, u32[]{:S(2)}) copy-start(f32[256,32,128]{2,0,1:T(8,128)} %fusion.12) | copy-start | bytes 12582916
  230.4 6.0 %copy-start.6 = (f32[256,32,128]{2,0,1:T(8,128)S(1)}, f32[256,32,128]{2,0,1:T(8,128)}, u32[]{:S(2)}) copy-start(f32[256,32,128]{2,0,1:T(8,128)} %get-tuple-element.20) | copy-start | bytes 12582916
  242.1 3.8 copy-start.4
  245.9 3.8 copy-start.5
  257.7 5.6 %copy-start.7 = (f32[256,32,128]{2,0,1:T(8,128)S(1)}, f32[256,32,128]{2,0,1:T(8,128)}, u32[]{:S(2)}) copy-start(f32[256,32,128]{2,0,1:T(8,128)} %get-tuple-element.21) | copy-start | bytes 12582916
  274.9 7.0 %copy-start.10 = (f32[256,32,128]{2,0,1:T(8,128)S(1)}, f32[256,32,128]{2,0,1:T(8,128)}, u32[]{:S(2)}) copy-start(f32[256,32,128]{2,0,1:T(8,128)} %get-tuple-element.35) | copy-start | bytes 12582916
  289.0 0.9 copy-start.14
  289.0 0.9 copy-start.15
  318.5 2.2 copy-start.17
  324.7 106.2 %all-to-all-start.1 = ((bf16[256,8,256]{0,2,1:T(8,128)(2,1)}), bf16[256,8,256]{0,2,1:T(8,128)(2,1)}, u32[]{:S(2)}, u32[]{:S(2)}) async-start(bf16[256,8,256]{0,2,1:T(8,128)(2,1)} %bitcast.19), calls=%async_computation.1 | async-start | bytes 2097152 | tf_op jit(solution)/shard_map/all_to_all | solution.py:126
  387.2 4.5 %copy-start.13 = (bf16[256,2054]{0,1:T(8,128)(2,1)S(1)}, bf16[256,2054]{0,1:T(8,128)(2,1)}, u32[]{:S(2)}) copy-start(bf16[256,2054]{0,1:T(8,128)(2,1)} %slice_bitcast_fusion) | copy-start | bytes 3154948
  391.8 41.4 %copy-start.1 = (bf16[2048,128]{1,0:T(8,128)(2,1)S(1)}, bf16[2048,128]{1,0:T(8,128)(2,1)}, u32[]{:S(2)}) copy-start(bf16[2048,128]{1,0:T(8,128)(2,1)} %param.9) | copy-start | bytes 1572868
where the time goes:
time: 440 us; the launch traced here: 434 us
  matrix products  346 us (79%)
  local copies, waits for them, and re-layouts  46.6 us (11%)
  starting transfers between devices  15.9 us (4%)
  waiting for transfers between devices  9.3 us (2%)
  blocking collectives  8.36 us (2%)
  other arithmetic  5.68 us (1%)
    conv_general_dilated x6, matrix products, depthwise(): lax.conv_general_dilated(signal[None], taps[:, None, :], (1,), 'VALID', d...  122 us
    dot_general x3, matrix products, forward_dft(): jnp.einsum('ckq,qr->ckr', turned_re, sin_inner, precision=highest)  39.9 us
    dot_general x3, matrix products, forward_dft(): jnp.einsum('ckq,qr->ckr', turned_im, sin_inner, precision=highest)  30.2 us
    dot_general x3, matrix products, forward_dft(): jnp.einsum('ckq,qr->ckr', turned_re, cos_inner, precision=highest)  30 us
    dot_general x3, matrix products, forward_dft(): jnp.einsum('ckq,qr->ckr', turned_im, cos_inner, precision=highest)  26.9 us
    dot_general x2, matrix products, inverse_dft(): jnp.einsum('ckq,qr->ckr', spec_re, sin_inner, precision=highest)  17.2 us
    dot_general x3, matrix products, forward_dft(): real = jnp.einsum('kn,cnq->ckq', cos_outer, blocks, precision=highest)  15 us
    dot_general x2, matrix products, inverse_dft(): jnp.einsum('kn,ckq->cnq', sin_outer, turned_im, precision=highest)  13.8 us
  transfers between devices with their start and end apart: 3, of which 1 were waited for; matrix products, arithmetic and copies ran while one was open for 36% of the time, Pallas kernels for 0%

commit v1 on v0

--- a/solution.py
+++ b/solution.py
@@ -5,6 +5,18 @@
 from jax.sharding import PartitionSpec as P
 
 highest = lax.Precision.HIGHEST
+
+
+def exchange_directly(array, axis, split, join):
+    ways, here = (lax.axis_size(axis), lax.axis_index(axis))
+    width = array.shape[split] // ways
+    turned = jnp.roll(array, -here * width, axis=split)
+    got = [lax.slice_in_dim(turned, 0, width, axis=split)]
+    for far in range(1, ways):
+        sent = lax.slice_in_dim(turned, far * width, (far + 1) * width, axis=split)
+        got.append(lax.ppermute(sent, axis, [(d, (d + far) % ways) for d in range(ways)]))
+    line = jnp.concatenate(got[::-1], axis=join)
+    return jnp.roll(line, (here + 1) * got[0].shape[join], axis=join)
 
 
 def depthwise(signal, taps):
@@ -91,7 +103,7 @@
     inv_rms = lax.rsqrt(squares / (chans * lax.axis_size("ch")) + 1e-05)
     normed = (inputs32 * inv_rms[None, :] * norm_gain[:, None]).astype(jnp.bfloat16)
     arrived, grad_chan = (
-        lax.all_to_all(normed, "seq", split_axis=0, concat_axis=1, tiled=True),
+        exchange_directly(normed, "seq", 0, 1),
         lax.all_to_all(grad_out, "seq", split_axis=0, concat_axis=1, tiled=True),
     )
     group, length = arrived.shape

time: 440 us -> 427 us (0.970)
  starting transfers between devices: 15.9 us -> 30 us
  matrix products: 346 us -> 332 us
  local copies, waits for them, and re-layouts: 46.6 us -> 39.8 us
    ppermute x0 -> x7, starting transfers between devices: none -> 18.2 us  [exchange_directly(): lax.ppermute(sent, axis, [(d, (d + far) % ways) for d in range(ways)])]
    conv_general_dilated x6, matrix products: 122 us -> 112 us  [depthwise(): lax.conv_general_dilated(signal[None], taps[:, None, :], (1,), 'VALID', d...]
    all_to_all x1 -> x0, waiting for transfers between devices: 9.3 us -> none  [on_device(): lax.all_to_all(normed, 'seq', split_axis=0, concat_axis=1, tiled=True)]
    all_to_all x1 -> x0, starting transfers between devices: 5.81 us -> none  [on_device(): lax.all_to_all(normed, 'seq', split_axis=0, concat_axis=1, tiled=True)]
    ppermute x0 -> x7, waiting for transfers between devices: none -> 5.71 us  [exchange_directly(): lax.ppermute(sent, axis, [(d, (d + far) % ways) for d in range(ways)])]
    convert_element_type x4, local copies, waits for them, and re-layouts: 6.09 us -> 0.64 us  [on_device(): shorted_grad = depthwise(back_pad, medium_local).astype(jnp.bfloat16)]
  transfers between devices with their start and end apart: 3 -> 9, of which waited for: 1 -> 2; matrix products, arithmetic and copies ran while one was open for 36% -> 43% of each run, Pallas kernels for 0% -> 0%
where the time goes in v1:
time: 427 us; the launch traced here: 420 us
  matrix products  332 us (78%)
  local copies, waits for them, and re-layouts  39.8 us (9%)
  starting transfers between devices  30 us (7%)
  blocking collectives  6.73 us (2%)
  waiting for transfers between devices  5.72 us (1%)
    conv_general_dilated x6, matrix products, depthwise(): lax.conv_general_dilated(signal[None], taps[:, None, :], (1,), 'VALID', d...  112 us
    dot_general x3, matrix products, forward_dft(): jnp.einsum('ckq,qr->ckr', turned_re, sin_inner, precision=highest)  39.2 us
    dot_general x3, matrix products, forward_dft(): jnp.einsum('ckq,qr->ckr', turned_re, cos_inner, precision=highest)  31.5 us
    dot_general x3, matrix products, forward_dft(): jnp.einsum('ckq,qr->ckr', turned_im, cos_inner, precision=highest)  27.1 us
    dot_general x3, matrix products, forward_dft(): jnp.einsum('ckq,qr->ckr', turned_im, sin_inner, precision=highest)  27 us
    ppermute x7, starting transfers between devices, exchange_directly(): lax.ppermute(sent, axis, [(d, (d + far) % ways) for d in range(ways)])  18.2 us
    dot_general x2, matrix products, inverse_dft(): jnp.einsum('ckq,qr->ckr', spec_re, sin_inner, precision=highest)  17.1 us
    dot_general x3, matrix products, forward_dft(): real = jnp.einsum('kn,cnq->ckq', cos_outer, blocks, precision=highest)  15 us
  transfers between devices with their start and end apart: 9, of which 2 were waited for; matrix products, arithmetic and copies ran while one was open for 43% of the time, Pallas kernels for 0%

profile of v1, /device:TPU:0, one launch (start us, length us, event | category | flops | bytes accessed | tf_op | source)
XLA Modules:
  0.0 419.7 jit_solution(14141013815121735997)
XLA Ops:
  0.7 7.4 %all-to-all-start = ((bf16[8,256,256]{2,1,0:T(8,128)(2,1)}), bf16[8,256,256]{2,1,0:T(8,128)(2,1)}, u32[]{:S(2)}, u32[]{:S(2)}) async-start(bf16[8,256,256]{2,1,0:T(8,128)(2,1)} %bitcast.205), calls=%async_computation | async-start | bytes 2097152 | tf_op jit(solution)/shard_map/all_to_all | solution.py:107
  8.1 1.5 copy.122
  9.8 6.7 %psum.7 = f32[256]{0:T(256)S(1)} all-reduce(f32[256]{0:T(256)S(1)} %fusion.44), channel_id=1, replica_groups=mesh['seq'=8,'ch'=4] {'ch'}, use_global_device_ids=true, to_apply=%region_1.0 | all-reduce | flops 256 | bytes 2048 | tf_op jit(solution)/shard_map/psum | solution.py:102
  17.6 4.5 %collective-permute-start = (bf16[256,256]{0,1:T(8,128)(2,1)S(1)}, bf16[256,256]{0,1:T(8,128)(2,1)S(1)}, u32[]{:S(2)}, u32[]{:S(2)}) collective-permute-start(bf16[256,256]{0,1:T(8,128)(2,1)S(1)} %get-tuple-element.40), channel_id=1, source_target_pairs={{0,28},{4,0},{8,4},{12,8},{16,12},{20,16},{24,20},{28,24},{1,29},{... | collective-permute-start | bytes 393224 | tf_op jit(solution)/shard_map/ppermute | solution.py:17
  22.6 2.5 collective-permute-start.3
  25.6 2.0 copy.147
  27.6 5.1 %fusion.172 = f32[32,256,128]{2,0,1:T(8,128)} fusion(f32[256,16,128]{2,1,0:T(8,128)S(1)} %bitcast.198), kind=kOutput, calls=%fused_computation.198 | convolution fusion | flops 201333760 | bytes 6291456 | tf_op jit(solution)/shard_map/kn,cnq->ckq/dot_general | solution.py:66
  32.7 5.2 %fusion.164 = f32[32,256,128]{2,0,1:T(8,128)} fusion(f32[256,16,128]{2,1,0:T(8,128)S(1)} %bitcast.199), kind=kOutput, calls=%fused_computation.190 | convolution fusion | flops 201333760 | bytes 6291456 | tf_op jit(solution)/shard_map/kn,cnq->ckq/dot_general | solution.py:67
  38.6 1.3 fusion.347
  41.2 2.1 collective-permute-start.5
  43.3 8.1 %collective-permute-start.6 = (bf16[256,256]{0,1:T(8,128)(2,1)S(1)}, bf16[256,256]{0,1:T(8,128)(2,1)S(1)}, u32[]{:S(2)}, u32[]{:S(2)}) collective-permute-start(bf16[256,256]{0,1:T(8,128)(2,1)S(1)} %get-tuple-element.34), channel_id=1, source_target_pairs={{0,4},{4,8},{8,12},{12,16},{16,20},{20,24},{24,28},{28,0},{1,5},{5... | collective-permute-start | bytes 393224 | tf_op jit(solution)/shard_map/ppermute | solution.py:17
  51.4 4.9 %collective-permute-done.3 = bf16[256,256]{0,1:T(8,128)(2,1)S(1)} collective-permute-done((bf16[256,256]{0,1:T(8,128)(2,1)S(1)}, bf16[256,256]{0,1:T(8,128)(2,1)S(1)}, u32[]{:S(2)}, u32[]{:S(2)}) %collective-permute-start.3) | collective-permute-done | bytes 131104 | tf_op jit(solution)/shard_map/ppermute | solution.py:17
  56.3 0.8 collective-permute-done.4
  57.8 1.2 slice_bitcast_fusion.1
  59.7 2.8 select_convert_fusion
  62.4 0.9 select_bitcast_fusion
  63.5 24.1 %fusion.66 = bf16[8,273,256]{2,0,1:T(8,128)(2,1)S(1)} fusion(bf16[256,1,128]{0,1,2:T(2,128)(2,1)S(1)} %copy.126, bf16[1,7,127,256]{3,1,2,0:T(8,128)(2,1)S(1)} %slice.60, bf16[1,8,273,256]{3,1,2,0:T(8,128)(2,1)S(1)} %select_bitcast_fusion), kind=kOutput, calls=%fused_computation.88 | convolution fusion | flops 148604928 | bytes 2757120 | tf_op jit(solution)/shard_map/conv_general_dilated | solution.py:23
  87.8 1.3 reshape.107
  89.2 2.3 slice.61
  91.4 1.9 copy.142
  93.4 3.8 fusion.167
  97.2 3.9 fusion.159
  101.3 4.3 %reshape.126 = bf16[1,2184,256]{2,0,1:T(2,128)(2,1)} reshape(bf16[8,273,256]{2,1,0:T(8,128)(2,1)S(1)} %copy.133) | data formatting | bytes 2236416 | tf_op jit(solution)/shard_map/convert_element_type | solution.py:115
  105.6 14.1 %fusion.93 = f32[256,32,128]{2,0,1:T(8,128)S(1)} fusion(f32[256,128,32]{1,2,0:T(8,128)} %fusion.167, f32[256,128,32]{1,2,0:T(8,128)} %fusion.159, f32[32,128]{1,0:T(8,128)S(1)} %get-tuple-element.45, f32[32,128]{1,0:T(8,128)S(1)} %get-tuple-element.46), kind=kOutput, calls=%fused_computation.112 | convolution fusion | flops 1615036416 | bytes 12615680 | tf_op jit(solution)/shard_map/ckq,qr->ckr/dot_general | solution.py:70
  119.8 12.9 %fusion.89 = f32[256,32,128]{2,0,1:T(8,128)} fusion(f32[256,128,32]{1,2,0:T(8,128)S(1)} %copy-done.2, f32[256,128,32]{1,2,0:T(8,128)S(1)} %copy-done.3, f32[32,128]{1,0:T(8,128)S(1)} %get-tuple-element.45, f32[32,128]{1,0:T(8,128)S(1)} %get-tuple-element.46), kind=kOutput, calls=%fused_computation.111 | convolution fusion | flops 1615036416 | bytes 12615680 | tf_op jit(solution)/shard_map/ckq,qr->ckr/dot_general | solution.py:73
  132.7 13.0 %convolution_add_fusion.1 = f32[256,32,128]{2,0,1:T(8,128)} fusion(f32[256,32,128]{2,0,1:T(8,128)S(1)} %fusion.93, f32[256,128,32]{1,2,0:T(8,128)S(1)} %copy-done.2, f32[256,128,32]{1,2,0:T(8,128)S(1)} %copy-done.3, f32[32,128]{1,0:T(8,128)S(1)} %get-tuple-element.45, f32[32,128]{1,0:T(8,128)S(1)} %get-tuple-element.46), kind=kOutput, calls=%fused_computation.62 | convolution fusion | flops 1616084992 | bytes 16809984 | tf_op jit(solution)/shard_map/ckq,qr->ckr/dot_general | solution.py:70
  145.7 1.8 copy.106
  147.5 1.6 reshape.84
  149.1 3.3 fusion.162
  152.4 6.0 %add_bitcast_fusion = (f32[256,32,128]{2,1,0:T(8,128)S(1)}, f32[256,32,128]{2,1,0:T(8,128)S(1)}, f32[256,32,128]{2,1,0:T(8,128)S(1)}, f32[256,32,128]{2,1,0:T(8,128)S(1)}) fusion(f32[32,256,128]{2,0,1:T(8,128)S(1)} %fusion.162, f32[32,128]{1,0:T(8,128)S(1)} %get-tuple-element.45, f32[32,128]{1,0:T(8,128)S(1)} %get-tuple-element.46, ...), kind=kOutput, calls=%fused_computation.24 | convolution fusion | flops 216013824 | bytes 30441472 | tf_op jit(solution)/shard_map/kn,cnq->ckq/dot_general | solution.py:66
  158.4 7.0 %fusion.12 = f32[256,32,128]{2,0,1:T(8,128)S(1)} fusion(f32[256,32,128]{2,1,0:T(8,128)S(1)} %get-tuple-element.29), kind=kOutput, calls=%fused_computation.29 | convolution fusion | flops 1610842112 | bytes 8388608 | tf_op jit(solution)/shard_map/ckq,qr->ckr/dot_general | solution.py:70
  165.4 7.0 %fusion.10 = f32[256,32,128]{2,0,1:T(8,128)S(1)} fusion(f32[256,32,128]{2,1,0:T(8,128)S(1)} %get-tuple-element.29), kind=kOutput, calls=%fused_computation.27 | convolution fusion | flops 1610842112 | bytes 8388608 | tf_op jit(solution)/shard_map/ckq,qr->ckr/dot_general | solution.py:73
  172.4 7.2 %fusion.18 = f32[256,32,128]{2,0,1:T(8,128)S(1)} fusion(f32[256,32,128]{2,1,0:T(8,128)S(1)} %get-tuple-element.43), kind=kOutput, calls=%fused_computation.35 | convolution fusion | flops 1610842112 | bytes 8388608 | tf_op jit(solution)/shard_map/ckq,qr->ckr/dot_general | solution.py:73
  179.6 7.0 %fusion.20 = f32[256,32,128]{2,0,1:T(8,128)S(1)} fusion(f32[256,32,128]{2,1,0:T(8,128)S(1)} %get-tuple-element.43), kind=kOutput, calls=%fused_computation.37 | convolution fusion | flops 1610842112 | bytes 8388608 | tf_op jit(solution)/shard_map/ckq,qr->ckr/dot_general | solution.py:70
  186.6 8.8 %fusion.36 = f32[256,32,128]{2,0,1:T(8,128)} fusion(f32[256,32,128]{2,0,1:T(8,128)S(1)} %fusion.12, f32[256,32,128]{2,1,0:T(8,128)S(1)} %get-tuple-element.28), kind=kOutput, calls=%fused_computation.57 | convolution fusion | flops 1611890688 | bytes 12582912 | tf_op jit(solution)/shard_map/ckq,qr->ckr/dot_general | solution.py:70
  195.3 8.5 %fusion.39 = f32[256,32,128]{2,0,1:T(8,128)} fusion(f32[256,32,128]{2,0,1:T(8,128)S(1)} %fusion.10, f32[256,32,128]{2,1,0:T(8,128)S(1)} %get-tuple-element.28), kind=kOutput, calls=%fused_computation.58 | convolution fusion | flops 1611890688 | bytes 12582912 | tf_op jit(solution)/shard_map/ckq,qr->ckr/dot_general | solution.py:73
  203.8 8.5 %fusion.33 = f32[256,32,128]{2,0,1:T(8,128)} fusion(f32[256,32,128]{2,0,1:T(8,128)S(1)} %fusion.18, f32[256,32,128]{2,1,0:T(8,128)S(1)} %get-tuple-element.44), kind=kOutput, calls=%fused_computation.56 | convolution fusion | flops 1611890688 | bytes 12582912 | tf_op jit(solution)/shard_map/ckq,qr->ckr/dot_general | solution.py:73
  212.3 8.6 %fusion.30 = f32[256,32,128]{2,0,1:T(8,128)} fusion(f32[256,32,128]{2,0,1:T(8,128)S(1)} %fusion.20, f32[256,32,128]{2,1,0:T(8,128)S(1)} %get-tuple-element.44), kind=kOutput, calls=%fused_computation.55 | convolution fusion | flops 1611890688 | bytes 12582912 | tf_op jit(solution)/shard_map/ckq,qr->ckr/dot_general | solution.py:70
  220.9 22.3 %multiply_subtract_fusion.1 = (f32[256,32,128]{2,0,1:T(8,128)}, f32[256,32,128]{2,0,1:T(8,128)}, f32[256,32,128]{2,0,1:T(8,128)}, f32[256,32,128]{2,0,1:T(8,128)}) fusion(f32[256,32,128]{2,0,1:T(8,128)} %fusion.36, f32[256,32,128]{2,0,1:T(8,128)} %convolution_add_fusion.1, f32[256,32,128]{2,0,1:T(8,128)} %fusion.39, f32[256,32,128]{2,0,1:T(8,128)} %fusion.33, ...), kind=kOutput, calls=%fused_computation.17 | convolution fusion | flops 1628667904 | bytes 50364416 | tf_op jit(solution)/shard_map/ckq,qr->ckr/dot_general | solution.py:73
  243.1 6.0 %fusion.112 = f32[256,32,128]{2,0,1:T(8,128)S(1)} fusion(f32[256,32,128]{2,0,1:T(8,128)} %get-tuple-element.21), kind=kOutput, calls=%fused_computation.136 | convolution fusion | flops 1610842112 | bytes 8388608 | tf_op jit(solution)/shard_map/ckq,qr->ckr/dot_general | solution.py:82
  249.2 5.9 %fusion.110 = f32[256,32,128]{2,0,1:T(8,128)} fusion(f32[256,32,128]{2,0,1:T(8,128)S(1)} %copy-done.6), kind=kOutput, calls=%fused_computation.134 | convolution fusion | flops 1610842112 | bytes 8388608 | tf_op jit(solution)/shard_map/ckq,qr->ckr/dot_general | solution.py:85
  255.1 3.8 convolution_subtract_fusion
  258.9 3.8 fusion.118
  262.7 3.8 fusion.116
  266.5 4.0 convolution_subtract_fusion.2
  270.5 5.5 %convolution_add_fusion.2 = f32[256,32,128]{2,0,1:T(8,128)} fusion(f32[256,32,128]{2,0,1:T(8,128)S(1)} %fusion.116, f32[256,32,128]{2,0,1:T(8,128)S(1)} %copy-done.4), kind=kOutput, calls=%fused_computation.63 | convolution fusion | flops 1611890688 | bytes 12582912 | tf_op jit(solution)/shard_map/ckq,qr->ckr/dot_general | solution.py:85
  276.0 11.6 %multiply_subtract_fusion = (f32[256,32,128]{2,0,1:T(8,128)}, f32[256,32,128]{2,0,1:T(8,128)}, f32[256,32,128]{2,0,1:T(8,128)}, f32[256,32,128]{2,0,1:T(8,128)}) fusion(f32[256,32,128]{2,0,1:T(8,128)S(1)} %convolution_subtract_fusion, f32[32,128]{1,0:T(8,128)S(1)} %get-tuple-element.45, f32[32,128]{1,0:T(8,128)S(1)} %get-tuple-element.46, ...), kind=kOutput, calls=%fused_computation.16 | convolution fusion | flops 1624473600 | bytes 37781504 | tf_op jit(solution)/shard_map/ckq,qr->ckr/dot_general | solution.py:85
  287.7 7.0 %fusion.6 = f32[256,128,16]{1,2,0:T(8,128)S(1)} fusion(f32[256,32,128]{2,0,1:T(8,128)} %get-tuple-element.41), kind=kOutput, calls=%fused_computation.11 | convolution fusion | flops 201333760 | bytes 6291456 | tf_op jit(solution)/shard_map/kn,ckq->cnq/dot_general | solution.py:90
  294.7 4.9 %fusion.69 = bf16[256,16,128]{2,1,0:T(8,128)(2,1)S(1)} fusion(f32[256,128,16]{1,2,0:T(8,128)S(1)} %fusion.6, f32[256,32,128]{2,0,1:T(8,128)S(1)} %copy-done.9), kind=kOutput, calls=%fused_computation.90 | convolution fusion | flops 202906624 | bytes 7340032 | tf_op jit(solution)/shard_map/kn,ckq->cnq/dot_general | solution.py:90
  299.6 0.8 copy.141
  300.4 1.3 convert_element_type.181
  302.6 28.8 %select_convert_fusion.1 = bf16[8,273,256]{2,0,1:T(8,128)(2,1)S(1)} fusion(bf16[256,1,128]{0,1,2:T(2,128)(2,1)S(1)} %copy-done.12, bf16[256,1,7,127]{0,2,3,1:T(8,128)(2,1)S(1)} %slice.48, bf16[256,1,8,273]{0,2,3,1:T(8,128)(2,1)S(1)} %copy.117, pred[8,273]{0,1:T(8,128)(4,1)S(1)} %copy-done.13), kind=kOutput, calls=%fused_computation.54 | convolution fusion | flops 149164032 | bytes 2759304 | tf_op jit(solution)/shard_map/conv_general_dilated | solution.py:23
  331.5 0.9 select_bitcast_fusion.1
  332.6 2.2 convolution_convert_fusion
  335.1 1.3 reshape.97
  336.4 2.3 slice.50
  338.7 4.4 %all-to-all-start.1 = ((bf16[256,8,256]{0,2,1:T(8,128)(2,1)}), bf16[256,8,256]{0,2,1:T(8,128)(2,1)}, u32[]{:S(2)}, u32[]{:S(2)}) async-start(bf16[256,8,256]{0,2,1:T(8,128)(2,1)} %bitcast.19), calls=%async_computation.1 | async-start | bytes 2097152 | tf_op jit(solution)/shard_map/all_to_all | solution.py:138
  343.1 7.0 %fusion.2 = f32[256,128,16]{1,2,0:T(8,128)S(1)} fusion(f32[256,32,128]{2,0,1:T(8,128)} %get-tuple-element.25), kind=kOutput, calls=%fused_computation.6 | convolution fusion | flops 201333760 | bytes 6291456 | tf_op jit(solution)/shard_map/kn,ckq->cnq/dot_general | solution.py:90
  350.1 4.9 %subtract_multiply_fusion = f32[256,128,16]{1,2,0:T(8,128)S(1)} fusion(f32[256,128,16]{1,2,0:T(8,128)S(1)} %fusion.2, f32[256,32,128]{2,0,1:T(8,128)S(1)} %copy-done.10), kind=kOutput, calls=%fused_computation.74 | convolution fusion | flops 202382336 | bytes 8388608 | tf_op jit(solution)/shard_map/kn,ckq->cnq/dot_general | solution.py:90
  355.0 2.2 copy.217
  357.3 3.7 copy.135
  361.0 25.4 %fusion.328 = f32[1,256,128]{1,0,2:T(1,128)S(1)} fusion(bf16[1,2184,256]{2,0,1:T(2,128)(2,1)} %reshape.126, bf16[256,1,2048]{0,1,2:T(2,128)(2,1)} %copy.135), kind=kOutput, calls=%fused_computation.347 | convolution fusion | flops 134217728 | bytes 2297856 | tf_op jit(solution)/shard_map/conv_general_dilated | solution.py:23
  388.0 28.6 %fusion.42 = f32[1,256,7]{1,0,2:T(1,128)S(1)} fusion(bf16[1,256,2054]{1,2,0:T(8,128)(2,1)} %slice_bitcast_fusion.1, bf16[256,1,2048]{0,2,1:T(8,128)(2,1)S(1)} %slice_bitcast_fusion.2), kind=kOutput, calls=%fused_computation.65 | convolution fusion | flops 7340032 | bytes 2107392 | tf_op jit(solution)/shard_map/conv_general_dilated | solution.py:23
  417.3 2.3 copy.121
  (100 shorter events, 9.7 us)
Async XLA Ops:
  0.6 37.3 %copy-start = (bf16[2048,128]{1,0:T(8,128)(2,1)S(1)}, bf16[2048,128]{1,0:T(8,128)(2,1)}, u32[]{:S(2)}) copy-start(bf16[2048,128]{1,0:T(8,128)(2,1)} %param.9) | copy-start | bytes 1572868
  0.6 15.9 %copy-start.15 = (f32[2048]{0:T(1024)S(1)}, f32[2048]{0:T(1024)}, u32[]{:S(2)}) copy-start(f32[2048]{0:T(1024)} %param.7) | copy-start | bytes 24580
  0.7 145.1 %all-to-all-start = ((bf16[8,256,256]{2,1,0:T(8,128)(2,1)}), bf16[8,256,256]{2,1,0:T(8,128)(2,1)}, u32[]{:S(2)}, u32[]{:S(2)}) async-start(bf16[8,256,256]{2,1,0:T(8,128)(2,1)} %bitcast.205), calls=%async_computation | async-start | bytes 2097152 | tf_op jit(solution)/shard_map/all_to_all | solution.py:107
  17.6 23.6 %collective-permute-start = (bf16[256,256]{0,1:T(8,128)(2,1)S(1)}, bf16[256,256]{0,1:T(8,128)(2,1)S(1)}, u32[]{:S(2)}, u32[]{:S(2)}) collective-permute-start(bf16[256,256]{0,1:T(8,128)(2,1)S(1)} %get-tuple-element.40), channel_id=1, source_target_pairs={{0,28},{4,0},{8,4},{12,8},{16,12},{20,16},{24,20},{28,24},{1,29},{... | collective-permute-start | bytes 393224 | tf_op jit(solution)/shard_map/ppermute | solution.py:17
  22.0 21.2 %collective-permute-start.1 = (bf16[256,256]{0,1:T(8,128)(2,1)S(1)}, bf16[256,256]{0,1:T(8,128)(2,1)S(1)}, u32[]{:S(2)}, u32[]{:S(2)}) collective-permute-start(bf16[256,256]{0,1:T(8,128)(2,1)S(1)} %get-tuple-element.39), channel_id=1, source_target_pairs={{0,24},{4,28},{8,0},{12,4},{16,8},{20,12},{24,16},{28,20},{1,25},{... | collective-permute-start | bytes 393224 | tf_op jit(solution)/shard_map/ppermute | solution.py:17
  22.6 28.8 %collective-permute-start.2 = (bf16[256,256]{0,1:T(8,128)(2,1)S(1)}, bf16[256,256]{0,1:T(8,128)(2,1)S(1)}, u32[]{:S(2)}, u32[]{:S(2)}) collective-permute-start(bf16[256,256]{0,1:T(8,128)(2,1)S(1)} %get-tuple-element.38), channel_id=1, source_target_pairs={{0,20},{4,24},{8,28},{12,0},{16,4},{20,8},{24,12},{28,16},{1,21},{... | collective-permute-start | bytes 393224 | tf_op jit(solution)/shard_map/ppermute | solution.py:17
  22.6 33.7 %collective-permute-start.3 = (bf16[256,256]{0,1:T(8,128)(2,1)S(1)}, bf16[256,256]{0,1:T(8,128)(2,1)S(1)}, u32[]{:S(2)}, u32[]{:S(2)}) collective-permute-start(bf16[256,256]{0,1:T(8,128)(2,1)S(1)} %get-tuple-element.37), channel_id=1, source_target_pairs={{0,16},{4,20},{8,24},{12,28},{16,0},{20,4},{24,8},{28,12},{1,17},{... | collective-permute-start | bytes 393224 | tf_op jit(solution)/shard_map/ppermute | solution.py:17
  25.1 32.0 %collective-permute-start.4 = (bf16[256,256]{0,1:T(8,128)(2,1)S(1)}, bf16[256,256]{0,1:T(8,128)(2,1)S(1)}, u32[]{:S(2)}, u32[]{:S(2)}) collective-permute-start(bf16[256,256]{0,1:T(8,128)(2,1)S(1)} %get-tuple-element.36), channel_id=1, source_target_pairs={{0,12},{4,16},{8,20},{12,24},{16,28},{20,0},{24,4},{28,8},{1,13},{... | collective-permute-start | bytes 393224 | tf_op jit(solution)/shard_map/ppermute | solution.py:17
  41.2 16.0 %collective-permute-start.5 = (bf16[256,256]{0,1:T(8,128)(2,1)S(1)}, bf16[256,256]{0,1:T(8,128)(2,1)S(1)}, u32[]{:S(2)}, u32[]{:S(2)}) collective-permute-start(bf16[256,256]{0,1:T(8,128)(2,1)S(1)} %get-tuple-element.35), channel_id=1, source_target_pairs={{0,8},{4,12},{8,16},{12,20},{16,24},{20,28},{24,0},{28,4},{1,9},{5... | collective-permute-start | bytes 393224 | tf_op jit(solution)/shard_map/ppermute | solution.py:17
  43.3 13.9 %collective-permute-start.6 = (bf16[256,256]{0,1:T(8,128)(2,1)S(1)}, bf16[256,256]{0,1:T(8,128)(2,1)S(1)}, u32[]{:S(2)}, u32[]{:S(2)}) collective-permute-start(bf16[256,256]{0,1:T(8,128)(2,1)S(1)} %get-tuple-element.34), channel_id=1, source_target_pairs={{0,4},{4,8},{8,12},{12,16},{16,20},{20,24},{24,28},{28,0},{1,5},{5... | collective-permute-start | bytes 393224 | tf_op jit(solution)/shard_map/ppermute | solution.py:17
  57.8 1.9 copy-start.14
  105.6 14.2 %copy-start.2 = (f32[256,128,32]{1,2,0:T(8,128)S(1)}, f32[256,128,32]{1,2,0:T(8,128)}, u32[]{:S(2)}) copy-start(f32[256,128,32]{1,2,0:T(8,128)} %fusion.167) | copy-start | bytes 12582916
  105.6 14.2 %copy-start.3 = (f32[256,128,32]{1,2,0:T(8,128)S(1)}, f32[256,128,32]{1,2,0:T(8,128)}, u32[]{:S(2)}) copy-start(f32[256,128,32]{1,2,0:T(8,128)} %fusion.159) | copy-start | bytes 12582916
  149.1 3.3 copy-start.8
  243.1 6.0 %copy-start.6 = (f32[256,32,128]{2,0,1:T(8,128)S(1)}, f32[256,32,128]{2,0,1:T(8,128)}, u32[]{:S(2)}) copy-start(f32[256,32,128]{2,0,1:T(8,128)} %get-tuple-element.20) | copy-start | bytes 12582916
  255.1 3.8 copy-start.4
  258.9 3.8 copy-start.5
  270.5 5.5 %copy-start.7 = (f32[256,32,128]{2,0,1:T(8,128)S(1)}, f32[256,32,128]{2,0,1:T(8,128)}, u32[]{:S(2)}) copy-start(f32[256,32,128]{2,0,1:T(8,128)} %get-tuple-element.21) | copy-start | bytes 12582916
  287.7 7.0 %copy-start.9 = (f32[256,32,128]{2,0,1:T(8,128)S(1)}, f32[256,32,128]{2,0,1:T(8,128)}, u32[]{:S(2)}) copy-start(f32[256,32,128]{2,0,1:T(8,128)} %get-tuple-element.42) | copy-start | bytes 12582916
  301.7 0.9 copy-start.12
  301.7 0.9 copy-start.13
  331.5 1.2 copy-start.16
  338.7 78.6 %all-to-all-start.1 = ((bf16[256,8,256]{0,2,1:T(8,128)(2,1)}), bf16[256,8,256]{0,2,1:T(8,128)(2,1)}, u32[]{:S(2)}, u32[]{:S(2)}) async-start(bf16[256,8,256]{0,2,1:T(8,128)(2,1)} %bitcast.19), calls=%async_computation.1 | async-start | bytes 2097152 | tf_op jit(solution)/shard_map/all_to_all | solution.py:138
  343.1 7.0 %copy-start.10 = (f32[256,32,128]{2,0,1:T(8,128)S(1)}, f32[256,32,128]{2,0,1:T(8,128)}, u32[]{:S(2)}) copy-start(f32[256,32,128]{2,0,1:T(8,128)} %get-tuple-element.24) | copy-start | bytes 12582916
  355.0 2.2 copy-start.11
  388.0 31.5 %copy-start.1 = (bf16[2048,128]{1,0:T(8,128)(2,1)S(1)}, bf16[2048,128]{1,0:T(8,128)(2,1)}, u32[]{:S(2)}) copy-start(bf16[2048,128]{1,0:T(8,128)(2,1)} %param.9) | copy-start | bytes 1572868
